TPU v7x, 256 devices: a whole 4x4x8 slice. The times are simulated.
256 devices in a mesh: col: 64 (over z, x, core), rep: 4 (over y).
Axes of the slice: x: 4, y: 4, z: 8, core: 2. Of those that a mesh axis runs over, the one named last changes fastest.
Arguments:
- looked: bfloat16 [32768, 1024], P('rep', 'col'), may hold values from -6 to 6
- cotangent: bfloat16 [32768, 1024], P('rep', 'col'), may hold values from -16 to 16
- w_in: bfloat16 [1024, 4096], replicated, may hold values from -0.1875 to 0.1875
- w_out: bfloat16 [1024, 1024], replicated, may hold values from -0.1875 to 0.1875
- lengths: int32 [512], P('rep'), may hold values from 1 to 127, as said below
- owner: int32 [512], P('rep'), may hold values from 0 to 63, as said below
Outputs:
- d_looked: bfloat16 [32768, 1024], P('rep', 'col')
- d_w_out: float32 [1024, 1024], P('col')
Inputs may be any that keep to these rules, and one draw needn't show every extreme that they name: In each replica group's 128 users every owner appears exactly 2 times, and the lengths of an owner's users sum to exactly 128. The lengths of one replica group's users sum to 8192.
All inputs are finite; a program needn't handle non-finite values.
Results may differ from a plain program's by a relative error of at most 0.018.
Values may be sent and summed in bfloat16 or wider, within the bound.
No kernel may reach another device: no remote copies, remote signals or barrier semaphores. Data moves between devices by JAX's collectives and lax.ppermute only.
A program may use at most 64 MiB of HBM per device.

v0:
```python
import functools

import jax
import jax.numpy as jnp
from jax import lax
from jax.experimental import pallas as pl
from jax.experimental.pallas import tpu as pltpu
from jax.sharding import PartitionSpec as P

HEADS = 8
EPS = 1e-05
BF = jnp.bfloat16
F32 = jnp.float32
LANES = 128
CHUNKS = 8
IN_FLIGHT = 8
HALVES = ((2, 4, 6), (3, 5, 7))
GATES = (0, 1)
FWD_MIB = 38
USERS_AT_ONCE = 32
OWNERS_AT_ONCE = 8
MOVES_AT_ONCE = 16

SMEM = pl.BlockSpec(memory_space=pltpu.SMEM)
VMEM = pl.BlockSpec(memory_space=pltpu.VMEM)
ANY = pl.BlockSpec(memory_space=pl.ANY)
HBM = pl.BlockSpec(memory_space=pltpu.HBM)


def params(mib):
    return pltpu.CompilerParams(vmem_limit_bytes=mib << 20)


def core_index():
    return lax.axis_index("col") & 1


def shape(dims, dtype=BF):
    return jax.ShapeDtypeStruct(dims, dtype)


def dot(a, b, ca, cb):
    return lax.dot_general(a, b, (((ca,), (cb,)), ((), ())), preferred_element_type=F32)


def pack_kernel(len_hbm, own_hbm, x_hbm, c_hbm, out_ref, table, mine_hbm, x_ref, c_ref, tab, seen, mine, sems):
    users = len_hbm.shape[0]
    lens, owns = table.at[pl.ds(2 * users, users)], table.at[pl.ds(3 * users, users)]
    copies = [
        pltpu.make_async_copy(src, dst, sems.at[i])
        for i, (src, dst) in enumerate(((len_hbm, lens), (own_hbm, owns), (x_hbm, x_ref), (c_hbm, c_ref)))
    ]
    for copy in copies:
        copy.start()
    owners = users // 2
    last = x_ref.shape[1] - LANES
    for j in range(owners):
        seen[j] = 0
    copies[0].wait()
    copies[1].wait()

    def user(u, off):
        own = table[3 * users + u]
        length = table[2 * users + u]
        second = seen[own]
        seen[own] = 1
        start = second * (LANES - length)
        table[u] = off
        table[users + u] = start
        tab[second, own] = off - start
        tab[2 + second, own] = length
        return off + length

    lax.fori_loop(0, users, user, 0, unroll=USERS_AT_ONCE)
    mine[...] = jnp.full(mine.shape, tab[2, lax.axis_index("col")], jnp.int32)
    tell = pltpu.make_async_copy(mine, mine_hbm.at[pl.ds(0, mine.shape[0])], sems.at[4])
    tell.start()
    copies[2].wait()
    copies[3].wait()
    lane = lax.broadcasted_iota(jnp.int32, (16, LANES), 1)

    def owner(j, carry):
        both = []
        for k in range(2):
            first = tab[k, j]
            inside = first & (LANES - 1)
            base = pl.multiple_of(first - inside, LANES)
            after = pl.multiple_of(jnp.minimum(base + LANES, last), LANES)
            back = (LANES - inside) & (LANES - 1)
            low = lane >= inside
            both.append(
                [
                    pltpu.roll(jnp.where(low, ref[:, pl.ds(base, LANES)], ref[:, pl.ds(after, LANES)]), back, 1)
                    for ref in (x_ref, c_ref)
                ]
            )
        head = lane < tab[2, j]
        out_ref[j, 0:16, :] = jnp.where(head, both[0][0], both[1][0])
        out_ref[j, 16:32, :] = jnp.where(head, both[0][1], both[1][1])
        return carry

    lax.fori_loop(0, owners, owner, 0, unroll=OWNERS_AT_ONCE)
    tell.wait()


def unpack_kernel(table, got_ref, out_ref, wide):
    users = table.shape[0] // 4
    lane = lax.broadcasted_iota(jnp.int32, (16, LANES), 1)

    def user(u, carry):
        off = table[u]
        own = table[3 * users + u]
        inside = off & (LANES - 1)
        base = pl.multiple_of(off - inside, LANES)
        turn = (inside - table[users + u]) & (LANES - 1)
        moved = pltpu.roll(got_ref[own >> 1, pl.ds(pl.multiple_of((own & 1) * 16, 16), 16), :], turn, 1).astype(F32)
        end = inside + table[2 * users + u]
        pltpu.store(wide.at[:, pl.ds(base, LANES)], moved, mask=(lane >= inside) & (lane < end))
        pltpu.store(wide.at[:, pl.ds(base + LANES, LANES)], moved, mask=lane < end - LANES)
        return carry

    lax.fori_loop(0, users, user, 0, unroll=MOVES_AT_ONCE)
    out_ref[...] = wide[:, : out_ref.shape[1]].astype(BF)


def sigmoid(v):
    return 0.5 * jnp.tanh(0.5 * v) + 0.5


def norm_parts(v):
    center = v - jnp.mean(v, axis=-1, keepdims=True)
    rstd = lax.rsqrt(jnp.mean(center * center, axis=-1, keepdims=True) + EPS)
    return center * rstd, rstd


def norm_back(hat, rstd, d):
    return rstd * (d - jnp.mean(d, axis=-1, keepdims=True) - hat * jnp.mean(d * hat, axis=-1, keepdims=True))


def column_chunks(w_hbm, w_ref, sems, order):
    per = w_hbm.shape[1] // len(order)

    def copy(i):
        part = pl.ds(order[i] * per, per)
        return pltpu.make_async_copy(w_hbm.at[:, part], w_ref.at[:, part], sems.at[i])

    def start(i):
        if i < len(order):
            copy(i).start()

    def wait(i):
        copy(i).wait()
        start(i + IN_FLIGHT)
        return slice(order[i] * per, (order[i] + 1) * per)

    for i in range(IN_FLIGHT):
        start(i)
    return wait


def forward_kernel(mine_hbm, rc_ref, w_hbm, acts_ref, slope_ref, wts_ref, wslope_ref, ahat_ref, arstd_ref, keep_ref, swap_ref, w_in, mine, sems):
    width = rc_ref.shape[0] * 16
    rows = rc_ref.shape[2]
    tell = pltpu.make_async_copy(mine_hbm.at[pl.ds(0, mine.shape[0])], mine, sems.at[CHUNKS])
    tell.start()
    order = HALVES[0] + HALVES[1] + GATES
    wait = column_chunks(w_hbm, w_in, sems, order)
    x = rc_ref[:, 0:16, :].reshape(width, rows).T
    normed = norm_parts(x.astype(F32))[0].astype(BF)
    query = lax.broadcasted_iota(jnp.int32, (rows, rows), 0)
    key = lax.broadcasted_iota(jnp.int32, (rows, rows), 1)
    tell.wait()
    first = mine[0:1, :]
    allowed = ((query < first) == (key < first)) & (key <= query)
    each = width // HEADS
    scale = float(each) ** -0.5
    attended = []

    def project(*chunks):
        for part in [wait(i) for i in chunks]:
            pre = dot(normed, w_in[:, part], 1, 0)
            gate = sigmoid(pre)
            act = pre * gate
            acts_ref[:, part] = act.astype(BF)
            slope_ref[:, part] = (gate + act * (1.0 - gate)).astype(BF)

    for half in range(2):
        project(*range(3 * half, 3 * half + 3))
        for h in range(half * HEADS // 2, (half + 1) * HEADS // 2):
            v = acts_ref[:, width + h * each : width + (h + 1) * each]
            q = acts_ref[:, 2 * width + h * each : 2 * width + (h + 1) * each]
            k = acts_ref[:, 3 * width + h * each : 3 * width + (h + 1) * each]
            scores = dot(q, k, 1, 1) * scale
            gate = sigmoid(scores)
            weight = scores * gate
            kept = jnp.where(allowed, weight, 0.0).astype(BF)
            wts_ref[h] = kept
            wslope_ref[h] = jnp.where(allowed, (gate + weight * (1.0 - gate)) * scale, 0.0).astype(BF)
            attended.append(dot(kept, v, 1, 0))
    hat, rstd = norm_parts(jnp.concatenate(attended, axis=1))
    ahat_ref[...] = hat
    arstd_ref[...] = jnp.broadcast_to(rstd, arstd_ref.shape)
    project(6, 7)
    mixed = (hat * acts_ref[:, :width].astype(F32)).astype(BF).T.reshape(32, 2, 16, rows)
    even = core_index() == 0
    keep_ref[...] = jnp.where(even, mixed[:, 0], mixed[:, 1]).reshape(width // 2, rows)
    swap_ref[: width // 2] = jnp.where(even, mixed[:, 1], mixed[:, 0]).reshape(width // 2, rows)
    swap_ref[width // 2 :] = rc_ref[:, 16:32, :].reshape(width, rows)


def mixed_grad_kernel(rc_ref, w_out_ref, d_mixed_ref):
    cots = rc_ref[:, 16:32, :].reshape(-1, LANES)
    d_mixed_ref[...] = dot(cots, w_out_ref[...], 0, 1).astype(BF)


def product_kernel(rc_ref, own_ref, got_ref, order_hbm, *out_refs):
    half = own_ref.shape[0]
    up = 2 * (lax.axis_index("rep") & 1)
    right = (lax.axis_index("col") >> 1) & 1
    mixed = jnp.concatenate([own_ref[...], got_ref[:half]], axis=1)
    for to, out in zip((up + right, 3 - up - right, 2 - up + right, up + 1 - right), out_refs):
        left_part = rc_ref[pl.ds(to * 16, 16), 16:32, :].reshape(256, LANES)
        right_part = got_ref[pl.ds(pl.multiple_of(half + to * 256, 256), 256), :]
        term = dot(mixed, jnp.concatenate([left_part, right_part], axis=1), 1, 1).astype(BF)
        out[:, 0:16, :] = term[:, :LANES].reshape(32, 16, LANES)
        out[:, 16:32, :] = term[:, LANES:].reshape(32, 16, LANES)


def backward_kernel(rc_ref, d_mixed_ref, acts_ref, slope_ref, wts_ref, wslope_ref, ahat_ref, arstd_ref, w_in, keep_ref, swap_ref, d_pre):
    width = rc_ref.shape[0] * 16
    rows = rc_ref.shape[2]
    d_mixed = d_mixed_ref[...].astype(F32)
    hat = ahat_ref[...]
    d_pre[:, :width] = ((d_mixed * hat) * slope_ref[:, :width].astype(F32)).astype(BF)
    d_att = norm_back(hat, arstd_ref[:, 0:1], d_mixed * acts_ref[:, :width].astype(F32)).astype(BF)
    each = width // HEADS
    for h in range(HEADS):
        vs = slice(width + h * each, width + (h + 1) * each)
        qs = slice(2 * width + h * each, 2 * width + (h + 1) * each)
        ks = slice(3 * width + h * each, 3 * width + (h + 1) * each)
        da = d_att[:, h * each : (h + 1) * each]
        d_weight = dot(da, acts_ref[:, vs], 1, 1)
        d_score = (d_weight * wslope_ref[h].astype(F32)).astype(BF)
        d_pre[:, vs] = (dot(wts_ref[h], da, 0, 0) * slope_ref[:, vs].astype(F32)).astype(BF)
        d_pre[:, qs] = (dot(d_score, acts_ref[:, ks], 1, 0) * slope_ref[:, qs].astype(F32)).astype(BF)
        d_pre[:, ks] = (dot(d_score, acts_ref[:, qs], 0, 0) * slope_ref[:, ks].astype(F32)).astype(BF)
    d_normed = dot(d_pre[...], w_in[...], 1, 1)
    cots = rc_ref[:, 16:32, :].reshape(width, rows).T
    x = rc_ref[:, 0:16, :].reshape(width, rows).T
    normed, rstd = norm_parts(x.astype(F32))
    grad = norm_back(normed, rstd, d_normed) + cots.astype(F32)
    grad = grad.astype(BF).T.reshape(32, 2, 16, rows)
    even = core_index() == 0
    keep_ref[...] = jnp.where(even, grad[:, 0], grad[:, 1])
    swap_ref[...] = jnp.where(even, grad[:, 1], grad[:, 0])


def merge_kernel(keep_ref, swapped_ref, *refs):
    out_ref = refs[-1]
    core = core_index()
    out_ref[:, pl.ds(pl.multiple_of(core * 16, 16), 16), :] = keep_ref[...]
    out_ref[:, pl.ds(pl.multiple_of((1 - core) * 16, 16), 16), :] = swapped_ref[...]
    total = refs[0][...].astype(F32)
    for part in refs[1:-1]:
        total += part[...].astype(F32)
    out_ref[:, 32:64, :] = total.astype(BF)


def last_sum_kernel(got_ref, out_ref):
    for side in range(2):
        total = got_ref[side, 32:64, :].astype(F32)
        for i in range(side + 2, got_ref.shape[0], 2):
            total += got_ref[i, 32:64, :].astype(F32)
        out_ref[:, 2 * side * LANES : (2 * side + 1) * LANES] = total[0:16]
        out_ref[:, (2 * side + 1) * LANES : (2 * side + 2) * LANES] = total[16:32]


def join_kernel(mine_ref, one_ref, two_ref, three_ref, out_ref):
    half = mine_ref.shape[1]
    up = lax.axis_index("rep") & 1
    out_ref[:, pl.ds(pl.multiple_of(up * half, half), half)] = mine_ref[...] + two_ref[...]
    out_ref[:, pl.ds(pl.multiple_of((1 - up) * half, half), half)] = one_ref[...] + three_ref[...]


def partners(along_x, along_rep):
    pairs = []
    for i in range(64):
        way = (1, 3)[i % 2]
        for y in range(4):
            to = i ^ (2 * way if along_x else 0), y ^ (way if along_rep else 0)
            pairs.append((i * 4 + y, to[0] * 4 + to[1]))
    return pairs


def per_device(looked, cotangent, w_in, w_out, lengths, owner):
    cols = lax.axis_size("col")
    events, mine_cols = looked.shape
    width = w_out.shape[0]
    rows = events // cols
    users = lengths.shape[0]
    send, table, first = pl.pallas_call(
        pack_kernel,
        out_shape=(
            shape((cols, 2 * mine_cols, rows)),
            shape((4 * users,), jnp.int32),
            shape((16384, LANES), jnp.int32),
        ),
        in_specs=[HBM] * 4,
        out_specs=(VMEM, SMEM, HBM),
        scratch_shapes=[
            pltpu.VMEM((mine_cols, events), BF),
            pltpu.VMEM((mine_cols, events), BF),
            pltpu.SMEM((4, cols), jnp.int32),
            pltpu.SMEM((cols,), jnp.int32),
            pltpu.VMEM((8, LANES), jnp.int32),
            pltpu.SemaphoreType.DMA((5,)),
        ],
        compiler_params=params(60),
    )(lengths, owner, looked.T, cotangent.T)
    packed = lax.all_to_all(send, "col", split_axis=0, concat_axis=0, tiled=True)
    acts, slope, wts, wslope, ahat, arstd, keep, swap, w_near = pl.pallas_call(
        forward_kernel,
        out_shape=(
            shape((rows, 4 * width)),
            shape((rows, 4 * width)),
            shape((HEADS, rows, rows)),
            shape((HEADS, rows, rows)),
            shape((rows, width), F32),
            shape((rows, LANES), F32),
            shape((width // 2, rows)),
            shape((width + width // 2, rows)),
            shape(w_in.shape),
        ),
        in_specs=[HBM, VMEM, HBM],
        scratch_shapes=[pltpu.VMEM((8, LANES), jnp.int32), pltpu.SemaphoreType.DMA((CHUNKS + 1,))],
        compiler_params=params(FWD_MIB),
    )(first, packed, w_in)
    other_core = [(i, i ^ 1) for i in range(cols)]
    got = lax.ppermute(swap, "col", other_core)
    d_mixed = pl.pallas_call(mixed_grad_kernel, out_shape=shape((rows, width)), compiler_params=params(16))(packed, w_out)
    block = (cols // 2, 2 * mine_cols, LANES)
    terms = pl.pallas_call(
        product_kernel,
        out_shape=[shape(block)] * 4,
        in_specs=[VMEM, VMEM, VMEM, ANY],
        compiler_params=params(16),
    )(packed, keep, got, d_mixed)
    ways = (True, True), (False, True), (True, False)
    terms = [terms[0]] + [lax.ppermute(t, ("col", "rep"), partners(*way)) for t, way in zip(terms[1:], ways)]
    grad, swap = pl.pallas_call(
        backward_kernel,
        out_shape=[shape((cols // 2, mine_cols, rows))] * 2,
        in_specs=[VMEM] * 9,
        scratch_shapes=[pltpu.VMEM((rows, 4 * width), BF)],
        compiler_params=params(16),
    )(packed, d_mixed, acts, slope, wts, wslope, ahat, arstd, w_near)
    swapped = lax.ppermute(swap, "col", other_core)
    merged = pl.pallas_call(
        merge_kernel,
        out_shape=shape((cols // 2, 4 * mine_cols, rows)),
        in_specs=[VMEM] * 6,
        compiler_params=params(16),
    )(grad, swapped, *terms)
    same_core = [list(range(core, cols, 2)) for core in range(2)]
    back = lax.all_to_all(merged, "col", split_axis=0, concat_axis=0, axis_index_groups=same_core, tiled=True)
    mine = pl.pallas_call(last_sum_kernel, out_shape=shape((mine_cols, width // 2), F32), compiler_params=params(16))(back)
    parts = [mine] + [lax.ppermute(mine, "rep", [(i, i ^ k) for i in range(4)]) for k in range(1, 4)]
    d_looked = pl.pallas_call(
        unpack_kernel,
        out_shape=shape((mine_cols, events)),
        in_specs=[SMEM, VMEM],
        scratch_shapes=[pltpu.VMEM((mine_cols, events + LANES), F32)],
        compiler_params=params(16),
    )(table, back)
    d_w_out = pl.pallas_call(
        join_kernel, out_shape=shape((mine_cols, width), F32), in_specs=[VMEM] * 4, compiler_params=params(16)
    )(*parts)
    return (d_looked.T, d_w_out)


def solution(mesh):
    placed = (P("rep", "col"), P("rep", "col"), P(), P(), P("rep"), P("rep"))
    return jax.shard_map(
        per_device,
        mesh=mesh,
        in_specs=placed,
        out_specs=(P("rep", "col"), P("col", None)),
        check_vma=False,
    )
```

profile of v0, /device:TPU:2, one launch (start us, length us, event | category | flops | bytes accessed | tf_op | source)
XLA Modules:
  0.0 85.9 jit_solution(11182473800376256620)
XLA Ops:
  0.6 3.9 %shard_map.77 = (bf16[64,32,128]{2,1,0:T(8,128)(2,1)}, s32[512]{0:T(512)}, s32[16384,128]{1,0:T(8,128)}) custom-call(s32[128]{0:T(128)} %len_hbm.1, s32[128]{0:T(128)} %own_hbm.1, bf16[16,8192]{1,0:T(8,128)(2,1)} %bitcast.4, bf16[16,8192]{1,0:T(8,128)(2,1)} %bitcast.5), custom_call_target="tpu_custom_call" | custom-call | tf_op jit(solution)/shard_map/pallas_call | solution.py:301
  4.5 29.6 %all_to_all.10.rc_ref = bf16[64,32,128]{2,1,0:T(8,128)(2,1)S(1)} all-to-all(bf16[64,32,128]{2,1,0:T(8,128)(2,1)} %get-tuple-element.21), channel_id=1, replica_groups=mesh['col'=64,'rep'=4] {'col'}, dimensions={0} | all-to-all | bytes 1048576 | tf_op jit(solution)/shard_map/all_to_all | solution.py:320
  34.1 0.0 copy-start
  34.1 5.5 %shard_map.79 = (bf16[128,4096]{1,0:T(8,128)(2,1)S(1)}, bf16[128,4096]{1,0:T(8,128)(2,1)S(1)}, bf16[8,128,128]{2,1,0:T(8,128)(2,1)S(1)}, bf16[8,128,128]{2,1,0:T...) custom-call(s32[16384,128]{1,0:T(8,128)} %get-tuple-element.22.mine_, ...), custom_call_target="tpu_custom_call" | custom-call | tf_op jit(solution)/shard_map/pallas_call | solution.py:321
  39.6 0.1 collective-permute-start.1
  39.7 0.0 copy-done
  39.7 0.8 shard_map.78.d_mixed_ref.order_hbm
  40.5 0.9 %collective-permute-done.1.got_ref = bf16[1536,128]{1,0:T(8,128)(2,1)S(1)} collective-permute-done((bf16[1536,128]{1,0:T(8,128)(2,1)S(1)}, bf16[1536,128]{1,0:T(8,128)(2,1)S(1)}, u32[]{:S(2)}, u32[]{:S(2)}) %collective-permute-start.1) | collective-permute-done | bytes 393248 | tf_op jit(solution)/shard_map/ppermute | solution.py:339
  41.4 0.0 copy-start.1
  41.4 0.5 shard_map.81
  41.9 1.7 %collective-permute-start.2 = (bf16[32,32,128]{2,1,0:T(8,128)(2,1)S(1)}, bf16[32,32,128]{2,1,0:T(8,128)(2,1)S(1)}, u32[]{:S(2)}, u32[]{:S(2)}) collective-permute-start(bf16[32,32,128]{2,1,0:T(8,128)(2,1)S(1)} %get-tuple-element.35), channel_id=1, source_target_pairs={{0,9},{1,8},{2,11},{3,10},{4,31},{5,30},{6,29},{7,28},{8,1},{9,0},... | collective-permute-start | bytes 786440 | tf_op jit(solution)/shard_map/ppermute | solution.py:349
  43.5 0.4 collective-permute-start.3
  44.0 1.5 %collective-permute-start.4 = (bf16[32,32,128]{2,1,0:T(8,128)(2,1)S(1)}, bf16[32,32,128]{2,1,0:T(8,128)(2,1)S(1)}, u32[]{:S(2)}, u32[]{:S(2)}) collective-permute-start(bf16[32,32,128]{2,1,0:T(8,128)(2,1)S(1)} %get-tuple-element.37), channel_id=1, source_target_pairs={{0,8},{1,9},{2,10},{3,11},{4,28},{5,29},{6,30},{7,31},{8,0},{9,1},... | collective-permute-start | bytes 786440 | tf_op jit(solution)/shard_map/ppermute | solution.py:349
  45.5 4.4 %shard_map.80 = (bf16[32,16,128]{2,1,0:T(8,128)(2,1)S(1)}, bf16[32,16,128]{2,1,0:T(8,128)(2,1)S(1)}) custom-call(bf16[64,32,128]{2,1,0:T(8,128)(2,1)S(1)} %all_to_all.10.rc_ref, bf16[128,1024]{1,0:T(8,128)(2,1)S(1)} %shard_map.78.d_mixed_ref.order_hbm, bf16[128,4096]{1,0:T(8,128)(2,1)S(1)} %get-tuple-element.23.acts_ref, ...), custom_call_target="tpu_custom_call" | custom-call | tf_op jit(solution)/shard_map/pallas_call | solution.py:350
  49.9 0.8 collective-permute-start
  50.6 1.0 %collective-permute-done.swapped_ref = bf16[32,16,128]{2,1,0:T(8,128)(2,1)S(1)} collective-permute-done((bf16[32,16,128]{2,1,0:T(8,128)(2,1)S(1)}, bf16[32,16,128]{2,1,0:T(8,128)(2,1)S(1)}, u32[]{:S(2)}, u32[]{:S(2)}) %collective-permute-start) | collective-permute-done | bytes 131104 | tf_op jit(solution)/shard_map/ppermute | solution.py:357
  51.6 0.0 collective-permute-done.2.refs_1_
  51.6 0.4 collective-permute-done.3.refs_2_
  52.1 0.2 collective-permute-done.4.refs_3_
  52.2 0.2 shard_map.82
  52.4 23.9 %all_to_all.11.got_ref = bf16[32,64,128]{2,1,0:T(8,128)(2,1)S(1)} all-to-all(bf16[32,64,128]{2,1,0:T(8,128)(2,1)S(1)} %shard_map.82), channel_id=1, replica_groups={{0,8,16,24,32,40,48,56,64,72,80,88,96,104,112,120,128,136,144,152,160,1..., dimensions={0} | all-to-all | bytes 1048576 | tf_op jit(solution)/shard_map/all_to_all | solution.py:365
  76.3 0.2 collective-permute-start.5
  76.6 3.5 %collective-permute-start.6 = (f32[16,512]{1,0:T(8,128)S(1)}, f32[16,512]{1,0:T(8,128)S(1)}, u32[]{:S(2)}, u32[]{:S(2)}) collective-permute-start(f32[16,512]{1,0:T(8,128)S(1)} %shard_map.84.mine_ref), channel_id=1, source_target_pairs={{0,2},{1,3},{2,0},{3,1},{4,6},{5,7},{6,4},{7,5},{8,10},{9,11},{10,... | collective-permute-start | bytes 98312 | tf_op jit(solution)/shard_map/ppermute | solution.py:367
  80.1 1.0 %collective-permute-start.7 = (f32[16,512]{1,0:T(8,128)S(1)}, f32[16,512]{1,0:T(8,128)S(1)}, u32[]{:S(2)}, u32[]{:S(2)}) collective-permute-start(f32[16,512]{1,0:T(8,128)S(1)} %shard_map.84.mine_ref), channel_id=1, source_target_pairs={{0,3},{1,2},{2,1},{3,0},{4,7},{5,6},{6,5},{7,4},{8,11},{9,10},{10,... | collective-permute-start | bytes 98312 | tf_op jit(solution)/shard_map/ppermute | solution.py:367
  81.1 0.0 copy-done.1
  81.1 2.6 %shard_map.83 = bf16[16,8192]{1,0:T(8,128)(2,1)} custom-call(s32[512]{0:T(512)S(1)} %copy-done.1, bf16[32,64,128]{2,1,0:T(8,128)(2,1)S(1)} %all_to_all.11.got_ref), custom_call_target="tpu_custom_call" | custom-call | tf_op jit(solution)/shard_map/pallas_call | solution.py:368
  83.7 0.0 collective-permute-done.5.one_ref
  83.7 0.0 collective-permute-done.6.two_ref
  83.8 1.5 %collective-permute-done.7.three_ref = f32[16,512]{1,0:T(8,128)S(1)} collective-permute-done((f32[16,512]{1,0:T(8,128)S(1)}, f32[16,512]{1,0:T(8,128)S(1)}, u32[]{:S(2)}, u32[]{:S(2)}) %collective-permute-start.7) | collective-permute-done | bytes 32800 | tf_op jit(solution)/shard_map/ppermute | solution.py:367
  85.2 0.6 shard_map.85
  (1 shorter events, 0.0 us)
Async XLA Ops:
  34.1 5.6 %copy-start = (bf16[1024,1024]{1,0:T(8,128)(2,1)S(1)}, bf16[1024,1024]{1,0:T(8,128)(2,1)}, u32[]{:S(2)}) copy-start(bf16[1024,1024]{1,0:T(8,128)(2,1)} %w_out_ref.1) | copy-start | bytes 6291460
  39.6 1.8 %collective-permute-start.1 = (bf16[1536,128]{1,0:T(8,128)(2,1)S(1)}, bf16[1536,128]{1,0:T(8,128)(2,1)S(1)}, u32[]{:S(2)}, u32[]{:S(2)}) collective-permute-start(bf16[1536,128]{1,0:T(8,128)(2,1)S(1)} %get-tuple-element.33), channel_id=1, source_target_pairs={{0,4},{4,0},{8,12},{12,8},{16,20},{20,16},{24,28},{28,24},{32,36},... | collective-permute-start | bytes 1179656 | tf_op jit(solution)/shard_map/ppermute | solution.py:339
  41.4 39.7 %copy-start.1 = (s32[512]{0:T(512)S(1)}, s32[512]{0:T(512)}, u32[]{:S(2)}) copy-start(s32[512]{0:T(512)} %get-tuple-element.20.table) | copy-start | bytes 6148
  41.9 9.7 %collective-permute-start.2 = (bf16[32,32,128]{2,1,0:T(8,128)(2,1)S(1)}, bf16[32,32,128]{2,1,0:T(8,128)(2,1)S(1)}, u32[]{:S(2)}, u32[]{:S(2)}) collective-permute-start(bf16[32,32,128]{2,1,0:T(8,128)(2,1)S(1)} %get-tuple-element.35), channel_id=1, source_target_pairs={{0,9},{1,8},{2,11},{3,10},{4,31},{5,30},{6,29},{7,28},{8,1},{9,0},... | collective-permute-start | bytes 786440 | tf_op jit(solution)/shard_map/ppermute | solution.py:349
  43.5 8.5 %collective-permute-start.3 = (bf16[32,32,128]{2,1,0:T(8,128)(2,1)S(1)}, bf16[32,32,128]{2,1,0:T(8,128)(2,1)S(1)}, u32[]{:S(2)}, u32[]{:S(2)}) collective-permute-start(bf16[32,32,128]{2,1,0:T(8,128)(2,1)S(1)} %get-tuple-element.36), channel_id=1, source_target_pairs={{0,1},{1,0},{2,3},{3,2},{4,7},{5,6},{6,5},{7,4},{8,9},{9,8},{10,11... | collective-permute-start | bytes 786440 | tf_op jit(solution)/shard_map/ppermute | solution.py:349
  44.0 8.2 %collective-permute-start.4 = (bf16[32,32,128]{2,1,0:T(8,128)(2,1)S(1)}, bf16[32,32,128]{2,1,0:T(8,128)(2,1)S(1)}, u32[]{:S(2)}, u32[]{:S(2)}) collective-permute-start(bf16[32,32,128]{2,1,0:T(8,128)(2,1)S(1)} %get-tuple-element.37), channel_id=1, source_target_pairs={{0,8},{1,9},{2,10},{3,11},{4,28},{5,29},{6,30},{7,31},{8,0},{9,1},... | collective-permute-start | bytes 786440 | tf_op jit(solution)/shard_map/ppermute | solution.py:349
  49.9 1.8 %collective-permute-start = (bf16[32,16,128]{2,1,0:T(8,128)(2,1)S(1)}, bf16[32,16,128]{2,1,0:T(8,128)(2,1)S(1)}, u32[]{:S(2)}, u32[]{:S(2)}) collective-permute-start(bf16[32,16,128]{2,1,0:T(8,128)(2,1)S(1)} %get-tuple-element.31), channel_id=1, source_target_pairs={{0,4},{4,0},{8,12},{12,8},{16,20},{20,16},{24,28},{28,24},{32,36},... | collective-permute-start | bytes 393224 | tf_op jit(solution)/shard_map/ppermute | solution.py:357
  76.3 7.4 %collective-permute-start.5 = (f32[16,512]{1,0:T(8,128)S(1)}, f32[16,512]{1,0:T(8,128)S(1)}, u32[]{:S(2)}, u32[]{:S(2)}) collective-permute-start(f32[16,512]{1,0:T(8,128)S(1)} %shard_map.84.mine_ref), channel_id=1, source_target_pairs={{0,1},{1,0},{2,3},{3,2},{4,5},{5,4},{6,7},{7,6},{8,9},{9,8},{10,11... | collective-permute-start | bytes 98312 | tf_op jit(solution)/shard_map/ppermute | solution.py:367
  76.6 7.2 %collective-permute-start.6 = (f32[16,512]{1,0:T(8,128)S(1)}, f32[16,512]{1,0:T(8,128)S(1)}, u32[]{:S(2)}, u32[]{:S(2)}) collective-permute-start(f32[16,512]{1,0:T(8,128)S(1)} %shard_map.84.mine_ref), channel_id=1, source_target_pairs={{0,2},{1,3},{2,0},{3,1},{4,6},{5,7},{6,4},{7,5},{8,10},{9,11},{10,... | collective-permute-start | bytes 98312 | tf_op jit(solution)/shard_map/ppermute | solution.py:367
  80.1 5.1 %collective-permute-start.7 = (f32[16,512]{1,0:T(8,128)S(1)}, f32[16,512]{1,0:T(8,128)S(1)}, u32[]{:S(2)}, u32[]{:S(2)}) collective-permute-start(f32[16,512]{1,0:T(8,128)S(1)} %shard_map.84.mine_ref), channel_id=1, source_target_pairs={{0,3},{1,2},{2,1},{3,0},{4,7},{5,6},{6,5},{7,4},{8,11},{9,10},{10,... | collective-permute-start | bytes 98312 | tf_op jit(solution)/shard_map/ppermute | solution.py:367
where the time goes:
time: 86.1 us; the launch traced here: 85.9 us
  blocking collectives  53.5 us (62%)
  Pallas kernels  18.5 us (21%)
  starting transfers between devices  9.23 us (11%)
  waiting for transfers between devices  3.93 us (5%)
    all_to_all x1, blocking collectives, per_device(): lax.all_to_all(send, 'col', split_axis=0, concat_axis=0, tiled=True)  29.6 us
    all_to_all x1, blocking collectives, per_device(): lax.all_to_all(merged, 'col', split_axis=0, concat_axis=0, axis_index_gro...  23.9 us
    pallas_call x1, Pallas kernels, per_device(): pl.pallas_call(forward_kernel, out_shape=(shape((rows, 4 * width)), shape...  5.52 us
    ppermute x3, starting transfers between devices, per_device(): lax.ppermute(mine, 'rep', [(i, i ^ k) for i in range(4)])  4.79 us
    pallas_call x1, Pallas kernels, per_device(): pl.pallas_call(backward_kernel, out_shape=[shape((cols // 2, mine_cols, r...  4.39 us
    pallas_call x1, Pallas kernels, per_device(): pl.pallas_call(pack_kernel, out_shape=(shape((cols, 2 * mine_cols, rows))...  3.86 us
    ppermute x3, starting transfers between devices, per_device(): lax.ppermute(t, ('col', 'rep'), partners(*way))  3.57 us
    pallas_call x1, Pallas kernels, per_device(): pl.pallas_call(unpack_kernel, out_shape=shape((mine_cols, events)), in_sp...  2.6 us
  transfers between devices with their start and end apart: 8, of which 5 were waited for; matrix products, arithmetic and copies ran while one was open for 0% of the time, Pallas kernels for 9%

commit v1 on v0

--- a/solution.py
+++ b/solution.py
@@ -275,7 +275,7 @@
         out_ref[:, (2 * side + 1) * LANES : (2 * side + 2) * LANES] = total[16:32]
 
 
-def join_kernel(mine_ref, one_ref, two_ref, three_ref, out_ref):
+def join_kernel(mine_ref, three_ref, two_ref, one_ref, out_ref):
     half = mine_ref.shape[1]
     up = lax.axis_index("rep") & 1
     out_ref[:, pl.ds(pl.multiple_of(up * half, half), half)] = mine_ref[...] + two_ref[...]
@@ -364,7 +364,7 @@
     same_core = [list(range(core, cols, 2)) for core in range(2)]
     back = lax.all_to_all(merged, "col", split_axis=0, concat_axis=0, axis_index_groups=same_core, tiled=True)
     mine = pl.pallas_call(last_sum_kernel, out_shape=shape((mine_cols, width // 2), F32), compiler_params=params(16))(back)
-    parts = [mine] + [lax.ppermute(mine, "rep", [(i, i ^ k) for i in range(4)]) for k in range(1, 4)]
+    three, two, one = [lax.ppermute(mine, "rep", [(i, i ^ k) for i in range(4)]) for k in (3, 2, 1)]
     d_looked = pl.pallas_call(
         unpack_kernel,
         out_shape=shape((mine_cols, events)),
@@ -374,7 +374,7 @@
     )(table, back)
     d_w_out = pl.pallas_call(
         join_kernel, out_shape=shape((mine_cols, width), F32), in_specs=[VMEM] * 4, compiler_params=params(16)
-    )(*parts)
+    )(mine, three, two, one)
     return (d_looked.T, d_w_out)
 
 

time: 86.1 us -> 84.9 us (0.986)
  no operation moved by 1% of the time
where the time goes in v1:
time: 84.9 us; the launch traced here: 84.7 us
  blocking collectives  53.5 us (63%)
  Pallas kernels  18.5 us (22%)
  starting transfers between devices  8.63 us (10%)
  waiting for transfers between devices  3.37 us (4%)
    all_to_all x1, blocking collectives, per_device(): lax.all_to_all(send, 'col', split_axis=0, concat_axis=0, tiled=True)  29.6 us
    all_to_all x1, blocking collectives, per_device(): lax.all_to_all(merged, 'col', split_axis=0, concat_axis=0, axis_index_gro...  23.9 us
    pallas_call x1, Pallas kernels, per_device(): pl.pallas_call(forward_kernel, out_shape=(shape((rows, 4 * width)), shape...  5.52 us
    pallas_call x1, Pallas kernels, per_device(): pl.pallas_call(backward_kernel, out_shape=[shape((cols // 2, mine_cols, r...  4.39 us
    ppermute x3, starting transfers between devices, per_device(): lax.ppermute(mine, 'rep', [(i, i ^ k) for i in range(4)])  4.18 us
    pallas_call x1, Pallas kernels, per_device(): pl.pallas_call(pack_kernel, out_shape=(shape((cols, 2 * mine_cols, rows))...  3.86 us
    ppermute x3, starting transfers between devices, per_device(): lax.ppermute(t, ('col', 'rep'), partners(*way))  3.57 us
    pallas_call x1, Pallas kernels, per_device(): pl.pallas_call(unpack_kernel, out_shape=shape((mine_cols, events)), in_sp...  2.6 us
  transfers between devices with their start and end apart: 8, of which 5 were waited for; matrix products, arithmetic and copies ran while one was open for 0% of the time, Pallas kernels for 9%

profile of v1, /device:TPU:2, one launch (start us, length us, event | category | flops | bytes accessed | tf_op | source)
XLA Modules:
  0.0 84.7 jit_solution(222388773834144717)
XLA Ops:
  0.6 3.9 %shard_map.77 = (bf16[64,32,128]{2,1,0:T(8,128)(2,1)}, s32[512]{0:T(512)}, s32[16384,128]{1,0:T(8,128)}) custom-call(s32[128]{0:T(128)} %len_hbm.1, s32[128]{0:T(128)} %own_hbm.1, bf16[16,8192]{1,0:T(8,128)(2,1)} %bitcast.4, bf16[16,8192]{1,0:T(8,128)(2,1)} %bitcast.5), custom_call_target="tpu_custom_call" | custom-call | tf_op jit(solution)/shard_map/pallas_call | solution.py:301
  4.5 29.6 %all_to_all.10.rc_ref = bf16[64,32,128]{2,1,0:T(8,128)(2,1)S(1)} all-to-all(bf16[64,32,128]{2,1,0:T(8,128)(2,1)} %get-tuple-element.21), channel_id=1, replica_groups=mesh['col'=64,'rep'=4] {'col'}, dimensions={0} | all-to-all | bytes 1048576 | tf_op jit(solution)/shard_map/all_to_all | solution.py:320
  34.1 0.0 copy-start
  34.1 5.5 %shard_map.79 = (bf16[128,4096]{1,0:T(8,128)(2,1)S(1)}, bf16[128,4096]{1,0:T(8,128)(2,1)S(1)}, bf16[8,128,128]{2,1,0:T(8,128)(2,1)S(1)}, bf16[8,128,128]{2,1,0:T...) custom-call(s32[16384,128]{1,0:T(8,128)} %get-tuple-element.22.mine_, ...), custom_call_target="tpu_custom_call" | custom-call | tf_op jit(solution)/shard_map/pallas_call | solution.py:321
  39.6 0.1 collective-permute-start.1
  39.7 0.0 copy-done
  39.7 0.8 shard_map.78.d_mixed_ref.order_hbm
  40.5 0.9 %collective-permute-done.1.got_ref = bf16[1536,128]{1,0:T(8,128)(2,1)S(1)} collective-permute-done((bf16[1536,128]{1,0:T(8,128)(2,1)S(1)}, bf16[1536,128]{1,0:T(8,128)(2,1)S(1)}, u32[]{:S(2)}, u32[]{:S(2)}) %collective-permute-start.1) | collective-permute-done | bytes 393248 | tf_op jit(solution)/shard_map/ppermute | solution.py:339
  41.4 0.0 copy-start.1
  41.4 0.5 shard_map.81
  41.9 1.7 %collective-permute-start.2 = (bf16[32,32,128]{2,1,0:T(8,128)(2,1)S(1)}, bf16[32,32,128]{2,1,0:T(8,128)(2,1)S(1)}, u32[]{:S(2)}, u32[]{:S(2)}) collective-permute-start(bf16[32,32,128]{2,1,0:T(8,128)(2,1)S(1)} %get-tuple-element.35), channel_id=1, source_target_pairs={{0,9},{1,8},{2,11},{3,10},{4,31},{5,30},{6,29},{7,28},{8,1},{9,0},... | collective-permute-start | bytes 786440 | tf_op jit(solution)/shard_map/ppermute | solution.py:349
  43.5 0.4 collective-permute-start.3
  44.0 1.5 %collective-permute-start.4 = (bf16[32,32,128]{2,1,0:T(8,128)(2,1)S(1)}, bf16[32,32,128]{2,1,0:T(8,128)(2,1)S(1)}, u32[]{:S(2)}, u32[]{:S(2)}) collective-permute-start(bf16[32,32,128]{2,1,0:T(8,128)(2,1)S(1)} %get-tuple-element.37), channel_id=1, source_target_pairs={{0,8},{1,9},{2,10},{3,11},{4,28},{5,29},{6,30},{7,31},{8,0},{9,1},... | collective-permute-start | bytes 786440 | tf_op jit(solution)/shard_map/ppermute | solution.py:349
  45.5 4.4 %shard_map.80 = (bf16[32,16,128]{2,1,0:T(8,128)(2,1)S(1)}, bf16[32,16,128]{2,1,0:T(8,128)(2,1)S(1)}) custom-call(bf16[64,32,128]{2,1,0:T(8,128)(2,1)S(1)} %all_to_all.10.rc_ref, bf16[128,1024]{1,0:T(8,128)(2,1)S(1)} %shard_map.78.d_mixed_ref.order_hbm, bf16[128,4096]{1,0:T(8,128)(2,1)S(1)} %get-tuple-element.23.acts_ref, ...), custom_call_target="tpu_custom_call" | custom-call | tf_op jit(solution)/shard_map/pallas_call | solution.py:350
  49.9 0.8 collective-permute-start
  50.6 1.0 %collective-permute-done.swapped_ref = bf16[32,16,128]{2,1,0:T(8,128)(2,1)S(1)} collective-permute-done((bf16[32,16,128]{2,1,0:T(8,128)(2,1)S(1)}, bf16[32,16,128]{2,1,0:T(8,128)(2,1)S(1)}, u32[]{:S(2)}, u32[]{:S(2)}) %collective-permute-start) | collective-permute-done | bytes 131104 | tf_op jit(solution)/shard_map/ppermute | solution.py:357
  51.6 0.0 collective-permute-done.2.refs_1_
  51.6 0.4 collective-permute-done.3.refs_2_
  52.1 0.2 collective-permute-done.4.refs_3_
  52.2 0.2 shard_map.82
  52.4 23.9 %all_to_all.11.got_ref = bf16[32,64,128]{2,1,0:T(8,128)(2,1)S(1)} all-to-all(bf16[32,64,128]{2,1,0:T(8,128)(2,1)S(1)} %shard_map.82), channel_id=1, replica_groups={{0,8,16,24,32,40,48,56,64,72,80,88,96,104,112,120,128,136,144,152,160,1..., dimensions={0} | all-to-all | bytes 1048576 | tf_op jit(solution)/shard_map/all_to_all | solution.py:365
  76.3 2.3 %collective-permute-start.5 = (f32[16,512]{1,0:T(8,128)S(1)}, f32[16,512]{1,0:T(8,128)S(1)}, u32[]{:S(2)}, u32[]{:S(2)}) collective-permute-start(f32[16,512]{1,0:T(8,128)S(1)} %shard_map.84.mine_ref), channel_id=1, source_target_pairs={{0,3},{1,2},{2,1},{3,0},{4,7},{5,6},{6,5},{7,4},{8,11},{9,10},{10,... | collective-permute-start | bytes 98312 | tf_op jit(solution)/shard_map/ppermute | solution.py:367
  78.6 0.0 collective-permute-start.6
  78.6 1.9 %collective-permute-start.7 = (f32[16,512]{1,0:T(8,128)S(1)}, f32[16,512]{1,0:T(8,128)S(1)}, u32[]{:S(2)}, u32[]{:S(2)}) collective-permute-start(f32[16,512]{1,0:T(8,128)S(1)} %shard_map.84.mine_ref), channel_id=1, source_target_pairs={{0,1},{1,0},{2,3},{3,2},{4,5},{5,4},{6,7},{7,6},{8,9},{9,8},{10,11... | collective-permute-start | bytes 98312 | tf_op jit(solution)/shard_map/ppermute | solution.py:367
  80.5 0.0 copy-done.1
  80.5 2.6 %shard_map.83 = bf16[16,8192]{1,0:T(8,128)(2,1)} custom-call(s32[512]{0:T(512)S(1)} %copy-done.1, bf16[32,64,128]{2,1,0:T(8,128)(2,1)S(1)} %all_to_all.11.got_ref), custom_call_target="tpu_custom_call" | custom-call | tf_op jit(solution)/shard_map/pallas_call | solution.py:368
  83.1 0.0 collective-permute-done.5.three_ref
  83.1 0.9 %collective-permute-done.6.two_ref = f32[16,512]{1,0:T(8,128)S(1)} collective-permute-done((f32[16,512]{1,0:T(8,128)S(1)}, f32[16,512]{1,0:T(8,128)S(1)}, u32[]{:S(2)}, u32[]{:S(2)}) %collective-permute-start.6) | collective-permute-done | bytes 32800 | tf_op jit(solution)/shard_map/ppermute | solution.py:367
  84.0 0.0 collective-permute-done.7.one_ref
  84.1 0.6 shard_map.85
  (1 shorter events, 0.0 us)
Async XLA Ops:
  34.1 5.6 %copy-start = (bf16[1024,1024]{1,0:T(8,128)(2,1)S(1)}, bf16[1024,1024]{1,0:T(8,128)(2,1)}, u32[]{:S(2)}) copy-start(bf16[1024,1024]{1,0:T(8,128)(2,1)} %w_out_ref.1) | copy-start | bytes 6291460
  39.6 1.8 %collective-permute-start.1 = (bf16[1536,128]{1,0:T(8,128)(2,1)S(1)}, bf16[1536,128]{1,0:T(8,128)(2,1)S(1)}, u32[]{:S(2)}, u32[]{:S(2)}) collective-permute-start(bf16[1536,128]{1,0:T(8,128)(2,1)S(1)} %get-tuple-element.33), channel_id=1, source_target_pairs={{0,4},{4,0},{8,12},{12,8},{16,20},{20,16},{24,28},{28,24},{32,36},... | collective-permute-start | bytes 1179656 | tf_op jit(solution)/shard_map/ppermute | solution.py:339
  41.4 39.1 %copy-start.1 = (s32[512]{0:T(512)S(1)}, s32[512]{0:T(512)}, u32[]{:S(2)}) copy-start(s32[512]{0:T(512)} %get-tuple-element.20.table) | copy-start | bytes 6148
  41.9 9.7 %collective-permute-start.2 = (bf16[32,32,128]{2,1,0:T(8,128)(2,1)S(1)}, bf16[32,32,128]{2,1,0:T(8,128)(2,1)S(1)}, u32[]{:S(2)}, u32[]{:S(2)}) collective-permute-start(bf16[32,32,128]{2,1,0:T(8,128)(2,1)S(1)} %get-tuple-element.35), channel_id=1, source_target_pairs={{0,9},{1,8},{2,11},{3,10},{4,31},{5,30},{6,29},{7,28},{8,1},{9,0},... | collective-permute-start | bytes 786440 | tf_op jit(solution)/shard_map/ppermute | solution.py:349
  43.5 8.5 %collective-permute-start.3 = (bf16[32,32,128]{2,1,0:T(8,128)(2,1)S(1)}, bf16[32,32,128]{2,1,0:T(8,128)(2,1)S(1)}, u32[]{:S(2)}, u32[]{:S(2)}) collective-permute-start(bf16[32,32,128]{2,1,0:T(8,128)(2,1)S(1)} %get-tuple-element.36), channel_id=1, source_target_pairs={{0,1},{1,0},{2,3},{3,2},{4,7},{5,6},{6,5},{7,4},{8,9},{9,8},{10,11... | collective-permute-start | bytes 786440 | tf_op jit(solution)/shard_map/ppermute | solution.py:349
  44.0 8.2 %collective-permute-start.4 = (bf16[32,32,128]{2,1,0:T(8,128)(2,1)S(1)}, bf16[32,32,128]{2,1,0:T(8,128)(2,1)S(1)}, u32[]{:S(2)}, u32[]{:S(2)}) collective-permute-start(bf16[32,32,128]{2,1,0:T(8,128)(2,1)S(1)} %get-tuple-element.37), channel_id=1, source_target_pairs={{0,8},{1,9},{2,10},{3,11},{4,28},{5,29},{6,30},{7,31},{8,0},{9,1},... | collective-permute-start | bytes 786440 | tf_op jit(solution)/shard_map/ppermute | solution.py:349
  49.9 1.8 %collective-permute-start = (bf16[32,16,128]{2,1,0:T(8,128)(2,1)S(1)}, bf16[32,16,128]{2,1,0:T(8,128)(2,1)S(1)}, u32[]{:S(2)}, u32[]{:S(2)}) collective-permute-start(bf16[32,16,128]{2,1,0:T(8,128)(2,1)S(1)} %get-tuple-element.31), channel_id=1, source_target_pairs={{0,4},{4,0},{8,12},{12,8},{16,20},{20,16},{24,28},{28,24},{32,36},... | collective-permute-start | bytes 393224 | tf_op jit(solution)/shard_map/ppermute | solution.py:357
  76.3 6.8 %collective-permute-start.5 = (f32[16,512]{1,0:T(8,128)S(1)}, f32[16,512]{1,0:T(8,128)S(1)}, u32[]{:S(2)}, u32[]{:S(2)}) collective-permute-start(f32[16,512]{1,0:T(8,128)S(1)} %shard_map.84.mine_ref), channel_id=1, source_target_pairs={{0,3},{1,2},{2,1},{3,0},{4,7},{5,6},{6,5},{7,4},{8,11},{9,10},{10,... | collective-permute-start | bytes 98312 | tf_op jit(solution)/shard_map/ppermute | solution.py:367
  78.6 5.4 %collective-permute-start.6 = (f32[16,512]{1,0:T(8,128)S(1)}, f32[16,512]{1,0:T(8,128)S(1)}, u32[]{:S(2)}, u32[]{:S(2)}) collective-permute-start(f32[16,512]{1,0:T(8,128)S(1)} %shard_map.84.mine_ref), channel_id=1, source_target_pairs={{0,2},{1,3},{2,0},{3,1},{4,6},{5,7},{6,4},{7,5},{8,10},{9,11},{10,... | collective-permute-start | bytes 98312 | tf_op jit(solution)/shard_map/ppermute | solution.py:367
  78.6 5.4 %collective-permute-start.7 = (f32[16,512]{1,0:T(8,128)S(1)}, f32[16,512]{1,0:T(8,128)S(1)}, u32[]{:S(2)}, u32[]{:S(2)}) collective-permute-start(f32[16,512]{1,0:T(8,128)S(1)} %shard_map.84.mine_ref), channel_id=1, source_target_pairs={{0,1},{1,0},{2,3},{3,2},{4,5},{5,4},{6,7},{7,6},{8,9},{9,8},{10,11... | collective-permute-start | bytes 98312 | tf_op jit(solution)/shard_map/ppermute | solution.py:367

commit v2 on v1

--- a/solution.py
+++ b/solution.py
@@ -185,7 +185,7 @@
             slope_ref[:, part] = (gate + act * (1.0 - gate)).astype(BF)
 
     for half in range(2):
-        project(*range(3 * half, 3 * half + 3))
+        project(*((0, 1, 2), (3, 4, 5, 6, 7))[half])
         for h in range(half * HEADS // 2, (half + 1) * HEADS // 2):
             v = acts_ref[:, width + h * each : width + (h + 1) * each]
             q = acts_ref[:, 2 * width + h * each : 2 * width + (h + 1) * each]
@@ -200,7 +200,6 @@
     hat, rstd = norm_parts(jnp.concatenate(attended, axis=1))
     ahat_ref[...] = hat
     arstd_ref[...] = jnp.broadcast_to(rstd, arstd_ref.shape)
-    project(6, 7)
     mixed = (hat * acts_ref[:, :width].astype(F32)).astype(BF).T.reshape(32, 2, 16, rows)
     even = core_index() == 0
     keep_ref[...] = jnp.where(even, mixed[:, 0], mixed[:, 1]).reshape(width // 2, rows)

time: 84.9 us -> 84.9 us (level)
  no operation moved by 1% of the time
where the time goes in v2:
time: 84.9 us; the launch traced here: 84.7 us
  blocking collectives  53.5 us (63%)
  Pallas kernels  18.5 us (22%)
  starting transfers between devices  8.62 us (10%)
  waiting for transfers between devices  3.38 us (4%)
    all_to_all x1, blocking collectives, per_device(): lax.all_to_all(send, 'col', split_axis=0, concat_axis=0, tiled=True)  29.6 us
    all_to_all x1, blocking collectives, per_device(): lax.all_to_all(merged, 'col', split_axis=0, concat_axis=0, axis_index_gro...  23.9 us
    pallas_call x1, Pallas kernels, per_device(): pl.pallas_call(forward_kernel, out_shape=(shape((rows, 4 * width)), shape...  5.52 us
    pallas_call x1, Pallas kernels, per_device(): pl.pallas_call(backward_kernel, out_shape=[shape((cols // 2, mine_cols, r...  4.39 us
    ppermute x3, starting transfers between devices, per_device(): lax.ppermute(mine, 'rep', [(i, i ^ k) for i in range(4)])  4.18 us
    pallas_call x1, Pallas kernels, per_device(): pl.pallas_call(pack_kernel, out_shape=(shape((cols, 2 * mine_cols, rows))...  3.86 us
    ppermute x3, starting transfers between devices, per_device(): lax.ppermute(t, ('col', 'rep'), partners(*way))  3.57 us
    pallas_call x1, Pallas kernels, per_device(): pl.pallas_call(unpack_kernel, out_shape=shape((mine_cols, events)), in_sp...  2.6 us
  transfers between devices with their start and end apart: 8, of which 5 were waited for; matrix products, arithmetic and copies ran while one was open for 0% of the time, Pallas kernels for 9%

profile of v2, /device:TPU:2, one launch (start us, length us, event | category | flops | bytes accessed | tf_op | source)
XLA Modules:
  0.0 84.7 jit_solution(14167752908099505575)
XLA Ops:
  0.6 3.9 %shard_map.77 = (bf16[64,32,128]{2,1,0:T(8,128)(2,1)}, s32[512]{0:T(512)}, s32[16384,128]{1,0:T(8,128)}) custom-call(s32[128]{0:T(128)} %len_hbm.1, s32[128]{0:T(128)} %own_hbm.1, bf16[16,8192]{1,0:T(8,128)(2,1)} %bitcast.4, bf16[16,8192]{1,0:T(8,128)(2,1)} %bitcast.5), custom_call_target="tpu_custom_call" | custom-call | tf_op jit(solution)/shard_map/pallas_call | solution.py:300
  4.5 29.6 %all_to_all.10.rc_ref = bf16[64,32,128]{2,1,0:T(8,128)(2,1)S(1)} all-to-all(bf16[64,32,128]{2,1,0:T(8,128)(2,1)} %get-tuple-element.21), channel_id=1, replica_groups=mesh['col'=64,'rep'=4] {'col'}, dimensions={0} | all-to-all | bytes 1048576 | tf_op jit(solution)/shard_map/all_to_all | solution.py:319
  34.1 0.0 copy-start
  34.1 5.5 %shard_map.79 = (bf16[128,4096]{1,0:T(8,128)(2,1)S(1)}, bf16[128,4096]{1,0:T(8,128)(2,1)S(1)}, bf16[8,128,128]{2,1,0:T(8,128)(2,1)S(1)}, bf16[8,128,128]{2,1,0:T...) custom-call(s32[16384,128]{1,0:T(8,128)} %get-tuple-element.22.mine_, ...), custom_call_target="tpu_custom_call" | custom-call | tf_op jit(solution)/shard_map/pallas_call | solution.py:320
  39.6 0.1 collective-permute-start.1
  39.7 0.0 copy-done
  39.7 0.8 shard_map.78.d_mixed_ref.order_hbm
  40.5 0.9 %collective-permute-done.1.got_ref = bf16[1536,128]{1,0:T(8,128)(2,1)S(1)} collective-permute-done((bf16[1536,128]{1,0:T(8,128)(2,1)S(1)}, bf16[1536,128]{1,0:T(8,128)(2,1)S(1)}, u32[]{:S(2)}, u32[]{:S(2)}) %collective-permute-start.1) | collective-permute-done | bytes 393248 | tf_op jit(solution)/shard_map/ppermute | solution.py:338
  41.4 0.0 copy-start.1
  41.4 0.5 shard_map.81
  41.9 1.6 %collective-permute-start.2 = (bf16[32,32,128]{2,1,0:T(8,128)(2,1)S(1)}, bf16[32,32,128]{2,1,0:T(8,128)(2,1)S(1)}, u32[]{:S(2)}, u32[]{:S(2)}) collective-permute-start(bf16[32,32,128]{2,1,0:T(8,128)(2,1)S(1)} %get-tuple-element.35), channel_id=1, source_target_pairs={{0,9},{1,8},{2,11},{3,10},{4,31},{5,30},{6,29},{7,28},{8,1},{9,0},... | collective-permute-start | bytes 786440 | tf_op jit(solution)/shard_map/ppermute | solution.py:348
  43.5 0.5 collective-permute-start.3
  44.0 1.5 %collective-permute-start.4 = (bf16[32,32,128]{2,1,0:T(8,128)(2,1)S(1)}, bf16[32,32,128]{2,1,0:T(8,128)(2,1)S(1)}, u32[]{:S(2)}, u32[]{:S(2)}) collective-permute-start(bf16[32,32,128]{2,1,0:T(8,128)(2,1)S(1)} %get-tuple-element.37), channel_id=1, source_target_pairs={{0,8},{1,9},{2,10},{3,11},{4,28},{5,29},{6,30},{7,31},{8,0},{9,1},... | collective-permute-start | bytes 786440 | tf_op jit(solution)/shard_map/ppermute | solution.py:348
  45.5 4.4 %shard_map.80 = (bf16[32,16,128]{2,1,0:T(8,128)(2,1)S(1)}, bf16[32,16,128]{2,1,0:T(8,128)(2,1)S(1)}) custom-call(bf16[64,32,128]{2,1,0:T(8,128)(2,1)S(1)} %all_to_all.10.rc_ref, bf16[128,1024]{1,0:T(8,128)(2,1)S(1)} %shard_map.78.d_mixed_ref.order_hbm, bf16[128,4096]{1,0:T(8,128)(2,1)S(1)} %get-tuple-element.23.acts_ref, ...), custom_call_target="tpu_custom_call" | custom-call | tf_op jit(solution)/shard_map/pallas_call | solution.py:349
  49.9 0.8 collective-permute-start
  50.6 1.0 %collective-permute-done.swapped_ref = bf16[32,16,128]{2,1,0:T(8,128)(2,1)S(1)} collective-permute-done((bf16[32,16,128]{2,1,0:T(8,128)(2,1)S(1)}, bf16[32,16,128]{2,1,0:T(8,128)(2,1)S(1)}, u32[]{:S(2)}, u32[]{:S(2)}) %collective-permute-start) | collective-permute-done | bytes 131104 | tf_op jit(solution)/shard_map/ppermute | solution.py:356
  51.6 0.0 collective-permute-done.2.refs_1_
  51.6 0.4 collective-permute-done.3.refs_2_
  52.1 0.2 collective-permute-done.4.refs_3_
  52.2 0.2 shard_map.82
  52.4 23.9 %all_to_all.11.got_ref = bf16[32,64,128]{2,1,0:T(8,128)(2,1)S(1)} all-to-all(bf16[32,64,128]{2,1,0:T(8,128)(2,1)S(1)} %shard_map.82), channel_id=1, replica_groups={{0,8,16,24,32,40,48,56,64,72,80,88,96,104,112,120,128,136,144,152,160,1..., dimensions={0} | all-to-all | bytes 1048576 | tf_op jit(solution)/shard_map/all_to_all | solution.py:364
  76.3 2.3 %collective-permute-start.5 = (f32[16,512]{1,0:T(8,128)S(1)}, f32[16,512]{1,0:T(8,128)S(1)}, u32[]{:S(2)}, u32[]{:S(2)}) collective-permute-start(f32[16,512]{1,0:T(8,128)S(1)} %shard_map.84.mine_ref), channel_id=1, source_target_pairs={{0,3},{1,2},{2,1},{3,0},{4,7},{5,6},{6,5},{7,4},{8,11},{9,10},{10,... | collective-permute-start | bytes 98312 | tf_op jit(solution)/shard_map/ppermute | solution.py:366
  78.6 0.0 collective-permute-start.6
  78.6 1.9 %collective-permute-start.7 = (f32[16,512]{1,0:T(8,128)S(1)}, f32[16,512]{1,0:T(8,128)S(1)}, u32[]{:S(2)}, u32[]{:S(2)}) collective-permute-start(f32[16,512]{1,0:T(8,128)S(1)} %shard_map.84.mine_ref), channel_id=1, source_target_pairs={{0,1},{1,0},{2,3},{3,2},{4,5},{5,4},{6,7},{7,6},{8,9},{9,8},{10,11... | collective-permute-start | bytes 98312 | tf_op jit(solution)/shard_map/ppermute | solution.py:366
  80.5 0.0 copy-done.1
  80.5 2.6 %shard_map.83 = bf16[16,8192]{1,0:T(8,128)(2,1)} custom-call(s32[512]{0:T(512)S(1)} %copy-done.1, bf16[32,64,128]{2,1,0:T(8,128)(2,1)S(1)} %all_to_all.11.got_ref), custom_call_target="tpu_custom_call" | custom-call | tf_op jit(solution)/shard_map/pallas_call | solution.py:367
  83.1 0.0 collective-permute-done.5.three_ref
  83.1 0.9 %collective-permute-done.6.two_ref = f32[16,512]{1,0:T(8,128)S(1)} collective-permute-done((f32[16,512]{1,0:T(8,128)S(1)}, f32[16,512]{1,0:T(8,128)S(1)}, u32[]{:S(2)}, u32[]{:S(2)}) %collective-permute-start.6) | collective-permute-done | bytes 32800 | tf_op jit(solution)/shard_map/ppermute | solution.py:366
  84.0 0.0 collective-permute-done.7.one_ref
  84.0 0.6 shard_map.85
  (1 shorter events, 0.0 us)
Async XLA Ops:
  34.1 5.6 %copy-start = (bf16[1024,1024]{1,0:T(8,128)(2,1)S(1)}, bf16[1024,1024]{1,0:T(8,128)(2,1)}, u32[]{:S(2)}) copy-start(bf16[1024,1024]{1,0:T(8,128)(2,1)} %w_out_ref.1) | copy-start | bytes 6291460
  39.6 1.8 %collective-permute-start.1 = (bf16[1536,128]{1,0:T(8,128)(2,1)S(1)}, bf16[1536,128]{1,0:T(8,128)(2,1)S(1)}, u32[]{:S(2)}, u32[]{:S(2)}) collective-permute-start(bf16[1536,128]{1,0:T(8,128)(2,1)S(1)} %get-tuple-element.33), channel_id=1, source_target_pairs={{0,4},{4,0},{8,12},{12,8},{16,20},{20,16},{24,28},{28,24},{32,36},... | collective-permute-start | bytes 1179656 | tf_op jit(solution)/shard_map/ppermute | solution.py:338
  41.4 39.1 %copy-start.1 = (s32[512]{0:T(512)S(1)}, s32[512]{0:T(512)}, u32[]{:S(2)}) copy-start(s32[512]{0:T(512)} %get-tuple-element.20.table) | copy-start | bytes 6148
  41.9 9.7 %collective-permute-start.2 = (bf16[32,32,128]{2,1,0:T(8,128)(2,1)S(1)}, bf16[32,32,128]{2,1,0:T(8,128)(2,1)S(1)}, u32[]{:S(2)}, u32[]{:S(2)}) collective-permute-start(bf16[32,32,128]{2,1,0:T(8,128)(2,1)S(1)} %get-tuple-element.35), channel_id=1, source_target_pairs={{0,9},{1,8},{2,11},{3,10},{4,31},{5,30},{6,29},{7,28},{8,1},{9,0},... | collective-permute-start | bytes 786440 | tf_op jit(solution)/shard_map/ppermute | solution.py:348
  43.5 8.5 %collective-permute-start.3 = (bf16[32,32,128]{2,1,0:T(8,128)(2,1)S(1)}, bf16[32,32,128]{2,1,0:T(8,128)(2,1)S(1)}, u32[]{:S(2)}, u32[]{:S(2)}) collective-permute-start(bf16[32,32,128]{2,1,0:T(8,128)(2,1)S(1)} %get-tuple-element.36), channel_id=1, source_target_pairs={{0,1},{1,0},{2,3},{3,2},{4,7},{5,6},{6,5},{7,4},{8,9},{9,8},{10,11... | collective-permute-start | bytes 786440 | tf_op jit(solution)/shard_map/ppermute | solution.py:348
  44.0 8.2 %collective-permute-start.4 = (bf16[32,32,128]{2,1,0:T(8,128)(2,1)S(1)}, bf16[32,32,128]{2,1,0:T(8,128)(2,1)S(1)}, u32[]{:S(2)}, u32[]{:S(2)}) collective-permute-start(bf16[32,32,128]{2,1,0:T(8,128)(2,1)S(1)} %get-tuple-element.37), channel_id=1, source_target_pairs={{0,8},{1,9},{2,10},{3,11},{4,28},{5,29},{6,30},{7,31},{8,0},{9,1},... | collective-permute-start | bytes 786440 | tf_op jit(solution)/shard_map/ppermute | solution.py:348
  49.9 1.7 %collective-permute-start = (bf16[32,16,128]{2,1,0:T(8,128)(2,1)S(1)}, bf16[32,16,128]{2,1,0:T(8,128)(2,1)S(1)}, u32[]{:S(2)}, u32[]{:S(2)}) collective-permute-start(bf16[32,16,128]{2,1,0:T(8,128)(2,1)S(1)} %get-tuple-element.31), channel_id=1, source_target_pairs={{0,4},{4,0},{8,12},{12,8},{16,20},{20,16},{24,28},{28,24},{32,36},... | collective-permute-start | bytes 393224 | tf_op jit(solution)/shard_map/ppermute | solution.py:356
  76.3 6.8 %collective-permute-start.5 = (f32[16,512]{1,0:T(8,128)S(1)}, f32[16,512]{1,0:T(8,128)S(1)}, u32[]{:S(2)}, u32[]{:S(2)}) collective-permute-start(f32[16,512]{1,0:T(8,128)S(1)} %shard_map.84.mine_ref), channel_id=1, source_target_pairs={{0,3},{1,2},{2,1},{3,0},{4,7},{5,6},{6,5},{7,4},{8,11},{9,10},{10,... | collective-permute-start | bytes 98312 | tf_op jit(solution)/shard_map/ppermute | solution.py:366
  78.6 5.4 %collective-permute-start.6 = (f32[16,512]{1,0:T(8,128)S(1)}, f32[16,512]{1,0:T(8,128)S(1)}, u32[]{:S(2)}, u32[]{:S(2)}) collective-permute-start(f32[16,512]{1,0:T(8,128)S(1)} %shard_map.84.mine_ref), channel_id=1, source_target_pairs={{0,2},{1,3},{2,0},{3,1},{4,6},{5,7},{6,4},{7,5},{8,10},{9,11},{10,... | collective-permute-start | bytes 98312 | tf_op jit(solution)/shard_map/ppermute | solution.py:366
  78.6 5.4 %collective-permute-start.7 = (f32[16,512]{1,0:T(8,128)S(1)}, f32[16,512]{1,0:T(8,128)S(1)}, u32[]{:S(2)}, u32[]{:S(2)}) collective-permute-start(f32[16,512]{1,0:T(8,128)S(1)} %shard_map.84.mine_ref), channel_id=1, source_target_pairs={{0,1},{1,0},{2,3},{3,2},{4,5},{5,4},{6,7},{7,6},{8,9},{9,8},{10,11... | collective-permute-start | bytes 98312 | tf_op jit(solution)/shard_map/ppermute | solution.py:366

commit v3 on v2

--- a/solution.py
+++ b/solution.py
@@ -274,7 +274,7 @@
         out_ref[:, (2 * side + 1) * LANES : (2 * side + 2) * LANES] = total[16:32]
 
 
-def join_kernel(mine_ref, three_ref, two_ref, one_ref, out_ref):
+def join_kernel(mine_ref, two_ref, three_ref, one_ref, out_ref):
     half = mine_ref.shape[1]
     up = lax.axis_index("rep") & 1
     out_ref[:, pl.ds(pl.multiple_of(up * half, half), half)] = mine_ref[...] + two_ref[...]
@@ -363,7 +363,7 @@
     same_core = [list(range(core, cols, 2)) for core in range(2)]
     back = lax.all_to_all(merged, "col", split_axis=0, concat_axis=0, axis_index_groups=same_core, tiled=True)
     mine = pl.pallas_call(last_sum_kernel, out_shape=shape((mine_cols, width // 2), F32), compiler_params=params(16))(back)
-    three, two, one = [lax.ppermute(mine, "rep", [(i, i ^ k) for i in range(4)]) for k in (3, 2, 1)]
+    two, three, one = [lax.ppermute(mine, "rep", [(i, i ^ k) for i in range(4)]) for k in (2, 3, 1)]
     d_looked = pl.pallas_call(
         unpack_kernel,
         out_shape=shape((mine_cols, events)),
@@ -373,7 +373,7 @@
     )(table, back)
     d_w_out = pl.pallas_call(
         join_kernel, out_shape=shape((mine_cols, width), F32), in_specs=[VMEM] * 4, compiler_params=params(16)
-    )(mine, three, two, one)
+    )(mine, two, three, one)
     return (d_looked.T, d_w_out)
 
 

time: 84.9 us -> 84 us (0.989)
  transfers between devices with their start and end apart: 8 -> 8, of which waited for: 5 -> 6; matrix products, arithmetic and copies ran while one was open for 0% -> 0% of each run, Pallas kernels for 9% -> 9%
where the time goes in v3:
time: 84 us; the launch traced here: 83.8 us
  blocking collectives  53.5 us (64%)
  Pallas kernels  18.5 us (22%)
  starting transfers between devices  8.01 us (10%)
  waiting for transfers between devices  3.1 us (4%)
    all_to_all x1, blocking collectives, per_device(): lax.all_to_all(send, 'col', split_axis=0, concat_axis=0, tiled=True)  29.6 us
    all_to_all x1, blocking collectives, per_device(): lax.all_to_all(merged, 'col', split_axis=0, concat_axis=0, axis_index_gro...  23.9 us
    pallas_call x1, Pallas kernels, per_device(): pl.pallas_call(forward_kernel, out_shape=(shape((rows, 4 * width)), shape...  5.52 us
    pallas_call x1, Pallas kernels, per_device(): pl.pallas_call(backward_kernel, out_shape=[shape((cols // 2, mine_cols, r...  4.39 us
    pallas_call x1, Pallas kernels, per_device(): pl.pallas_call(pack_kernel, out_shape=(shape((cols, 2 * mine_cols, rows))...  3.86 us
    ppermute x3, starting transfers between devices, per_device(): lax.ppermute(mine, 'rep', [(i, i ^ k) for i in range(4)])  3.58 us
    ppermute x3, starting transfers between devices, per_device(): lax.ppermute(t, ('col', 'rep'), partners(*way))  3.57 us
    pallas_call x1, Pallas kernels, per_device(): pl.pallas_call(unpack_kernel, out_shape=shape((mine_cols, events)), in_sp...  2.6 us
  transfers between devices with their start and end apart: 8, of which 6 were waited for; matrix products, arithmetic and copies ran while one was open for 0% of the time, Pallas kernels for 9%

profile of v3, /device:TPU:2, one launch (start us, length us, event | category | flops | bytes accessed | tf_op | source)
XLA Modules:
  0.0 83.8 jit_solution(12554030393330036337)
XLA Ops:
  0.6 3.9 %shard_map.77 = (bf16[64,32,128]{2,1,0:T(8,128)(2,1)}, s32[512]{0:T(512)}, s32[16384,128]{1,0:T(8,128)}) custom-call(s32[128]{0:T(128)} %len_hbm.1, s32[128]{0:T(128)} %own_hbm.1, bf16[16,8192]{1,0:T(8,128)(2,1)} %bitcast.4, bf16[16,8192]{1,0:T(8,128)(2,1)} %bitcast.5), custom_call_target="tpu_custom_call" | custom-call | tf_op jit(solution)/shard_map/pallas_call | solution.py:300
  4.5 29.6 %all_to_all.10.rc_ref = bf16[64,32,128]{2,1,0:T(8,128)(2,1)S(1)} all-to-all(bf16[64,32,128]{2,1,0:T(8,128)(2,1)} %get-tuple-element.21), channel_id=1, replica_groups=mesh['col'=64,'rep'=4] {'col'}, dimensions={0} | all-to-all | bytes 1048576 | tf_op jit(solution)/shard_map/all_to_all | solution.py:319
  34.1 0.0 copy-start
  34.1 5.5 %shard_map.79 = (bf16[128,4096]{1,0:T(8,128)(2,1)S(1)}, bf16[128,4096]{1,0:T(8,128)(2,1)S(1)}, bf16[8,128,128]{2,1,0:T(8,128)(2,1)S(1)}, bf16[8,128,128]{2,1,0:T...) custom-call(s32[16384,128]{1,0:T(8,128)} %get-tuple-element.22.mine_, ...), custom_call_target="tpu_custom_call" | custom-call | tf_op jit(solution)/shard_map/pallas_call | solution.py:320
  39.6 0.1 collective-permute-start.1
  39.7 0.0 copy-done
  39.7 0.8 shard_map.78.d_mixed_ref.order_hbm
  40.5 0.9 %collective-permute-done.1.got_ref = bf16[1536,128]{1,0:T(8,128)(2,1)S(1)} collective-permute-done((bf16[1536,128]{1,0:T(8,128)(2,1)S(1)}, bf16[1536,128]{1,0:T(8,128)(2,1)S(1)}, u32[]{:S(2)}, u32[]{:S(2)}) %collective-permute-start.1) | collective-permute-done | bytes 393248 | tf_op jit(solution)/shard_map/ppermute | solution.py:338
  41.4 0.0 copy-start.1
  41.4 0.5 shard_map.81
  41.9 1.6 %collective-permute-start.2 = (bf16[32,32,128]{2,1,0:T(8,128)(2,1)S(1)}, bf16[32,32,128]{2,1,0:T(8,128)(2,1)S(1)}, u32[]{:S(2)}, u32[]{:S(2)}) collective-permute-start(bf16[32,32,128]{2,1,0:T(8,128)(2,1)S(1)} %get-tuple-element.35), channel_id=1, source_target_pairs={{0,9},{1,8},{2,11},{3,10},{4,31},{5,30},{6,29},{7,28},{8,1},{9,0},... | collective-permute-start | bytes 786440 | tf_op jit(solution)/shard_map/ppermute | solution.py:348
  43.5 0.5 collective-permute-start.3
  44.0 1.5 %collective-permute-start.4 = (bf16[32,32,128]{2,1,0:T(8,128)(2,1)S(1)}, bf16[32,32,128]{2,1,0:T(8,128)(2,1)S(1)}, u32[]{:S(2)}, u32[]{:S(2)}) collective-permute-start(bf16[32,32,128]{2,1,0:T(8,128)(2,1)S(1)} %get-tuple-element.37), channel_id=1, source_target_pairs={{0,8},{1,9},{2,10},{3,11},{4,28},{5,29},{6,30},{7,31},{8,0},{9,1},... | collective-permute-start | bytes 786440 | tf_op jit(solution)/shard_map/ppermute | solution.py:348
  45.5 4.4 %shard_map.80 = (bf16[32,16,128]{2,1,0:T(8,128)(2,1)S(1)}, bf16[32,16,128]{2,1,0:T(8,128)(2,1)S(1)}) custom-call(bf16[64,32,128]{2,1,0:T(8,128)(2,1)S(1)} %all_to_all.10.rc_ref, bf16[128,1024]{1,0:T(8,128)(2,1)S(1)} %shard_map.78.d_mixed_ref.order_hbm, bf16[128,4096]{1,0:T(8,128)(2,1)S(1)} %get-tuple-element.23.acts_ref, ...), custom_call_target="tpu_custom_call" | custom-call | tf_op jit(solution)/shard_map/pallas_call | solution.py:349
  49.9 0.8 collective-permute-start
  50.6 1.0 %collective-permute-done.swapped_ref = bf16[32,16,128]{2,1,0:T(8,128)(2,1)S(1)} collective-permute-done((bf16[32,16,128]{2,1,0:T(8,128)(2,1)S(1)}, bf16[32,16,128]{2,1,0:T(8,128)(2,1)S(1)}, u32[]{:S(2)}, u32[]{:S(2)}) %collective-permute-start) | collective-permute-done | bytes 131104 | tf_op jit(solution)/shard_map/ppermute | solution.py:356
  51.6 0.0 collective-permute-done.2.refs_1_
  51.6 0.4 collective-permute-done.3.refs_2_
  52.1 0.2 collective-permute-done.4.refs_3_
  52.2 0.2 shard_map.82
  52.4 23.9 %all_to_all.11.got_ref = bf16[32,64,128]{2,1,0:T(8,128)(2,1)S(1)} all-to-all(bf16[32,64,128]{2,1,0:T(8,128)(2,1)S(1)} %shard_map.82), channel_id=1, replica_groups={{0,8,16,24,32,40,48,56,64,72,80,88,96,104,112,120,128,136,144,152,160,1..., dimensions={0} | all-to-all | bytes 1048576 | tf_op jit(solution)/shard_map/all_to_all | solution.py:364
  76.3 1.3 %collective-permute-start.5 = (f32[16,512]{1,0:T(8,128)S(1)}, f32[16,512]{1,0:T(8,128)S(1)}, u32[]{:S(2)}, u32[]{:S(2)}) collective-permute-start(f32[16,512]{1,0:T(8,128)S(1)} %shard_map.84.mine_ref), channel_id=1, source_target_pairs={{0,2},{1,3},{2,0},{3,1},{4,6},{5,7},{6,4},{7,5},{8,10},{9,11},{10,... | collective-permute-start | bytes 98312 | tf_op jit(solution)/shard_map/ppermute | solution.py:366
  77.7 1.6 %collective-permute-start.6 = (f32[16,512]{1,0:T(8,128)S(1)}, f32[16,512]{1,0:T(8,128)S(1)}, u32[]{:S(2)}, u32[]{:S(2)}) collective-permute-start(f32[16,512]{1,0:T(8,128)S(1)} %shard_map.84.mine_ref), channel_id=1, source_target_pairs={{0,3},{1,2},{2,1},{3,0},{4,7},{5,6},{6,5},{7,4},{8,11},{9,10},{10,... | collective-permute-start | bytes 98312 | tf_op jit(solution)/shard_map/ppermute | solution.py:366
  79.2 0.7 collective-permute-start.7
  79.9 0.0 copy-done.1
  79.9 2.6 %shard_map.83 = bf16[16,8192]{1,0:T(8,128)(2,1)} custom-call(s32[512]{0:T(512)S(1)} %copy-done.1, bf16[32,64,128]{2,1,0:T(8,128)(2,1)S(1)} %all_to_all.11.got_ref), custom_call_target="tpu_custom_call" | custom-call | tf_op jit(solution)/shard_map/pallas_call | solution.py:367
  82.5 0.0 collective-permute-done.5.two_ref
  82.5 0.2 collective-permute-done.6.three_ref
  82.8 0.4 collective-permute-done.7.one_ref
  83.2 0.6 shard_map.85
  (1 shorter events, 0.0 us)
Async XLA Ops:
  34.1 5.6 %copy-start = (bf16[1024,1024]{1,0:T(8,128)(2,1)S(1)}, bf16[1024,1024]{1,0:T(8,128)(2,1)}, u32[]{:S(2)}) copy-start(bf16[1024,1024]{1,0:T(8,128)(2,1)} %w_out_ref.1) | copy-start | bytes 6291460
  39.6 1.8 %collective-permute-start.1 = (bf16[1536,128]{1,0:T(8,128)(2,1)S(1)}, bf16[1536,128]{1,0:T(8,128)(2,1)S(1)}, u32[]{:S(2)}, u32[]{:S(2)}) collective-permute-start(bf16[1536,128]{1,0:T(8,128)(2,1)S(1)} %get-tuple-element.33), channel_id=1, source_target_pairs={{0,4},{4,0},{8,12},{12,8},{16,20},{20,16},{24,28},{28,24},{32,36},... | collective-permute-start | bytes 1179656 | tf_op jit(solution)/shard_map/ppermute | solution.py:338
  41.4 38.5 %copy-start.1 = (s32[512]{0:T(512)S(1)}, s32[512]{0:T(512)}, u32[]{:S(2)}) copy-start(s32[512]{0:T(512)} %get-tuple-element.20.table) | copy-start | bytes 6148
  41.9 9.7 %collective-permute-start.2 = (bf16[32,32,128]{2,1,0:T(8,128)(2,1)S(1)}, bf16[32,32,128]{2,1,0:T(8,128)(2,1)S(1)}, u32[]{:S(2)}, u32[]{:S(2)}) collective-permute-start(bf16[32,32,128]{2,1,0:T(8,128)(2,1)S(1)} %get-tuple-element.35), channel_id=1, source_target_pairs={{0,9},{1,8},{2,11},{3,10},{4,31},{5,30},{6,29},{7,28},{8,1},{9,0},... | collective-permute-start | bytes 786440 | tf_op jit(solution)/shard_map/ppermute | solution.py:348
  43.5 8.5 %collective-permute-start.3 = (bf16[32,32,128]{2,1,0:T(8,128)(2,1)S(1)}, bf16[32,32,128]{2,1,0:T(8,128)(2,1)S(1)}, u32[]{:S(2)}, u32[]{:S(2)}) collective-permute-start(bf16[32,32,128]{2,1,0:T(8,128)(2,1)S(1)} %get-tuple-element.36), channel_id=1, source_target_pairs={{0,1},{1,0},{2,3},{3,2},{4,7},{5,6},{6,5},{7,4},{8,9},{9,8},{10,11... | collective-permute-start | bytes 786440 | tf_op jit(solution)/shard_map/ppermute | solution.py:348
  44.0 8.2 %collective-permute-start.4 = (bf16[32,32,128]{2,1,0:T(8,128)(2,1)S(1)}, bf16[32,32,128]{2,1,0:T(8,128)(2,1)S(1)}, u32[]{:S(2)}, u32[]{:S(2)}) collective-permute-start(bf16[32,32,128]{2,1,0:T(8,128)(2,1)S(1)} %get-tuple-element.37), channel_id=1, source_target_pairs={{0,8},{1,9},{2,10},{3,11},{4,28},{5,29},{6,30},{7,31},{8,0},{9,1},... | collective-permute-start | bytes 786440 | tf_op jit(solution)/shard_map/ppermute | solution.py:348
  49.9 1.7 %collective-permute-start = (bf16[32,16,128]{2,1,0:T(8,128)(2,1)S(1)}, bf16[32,16,128]{2,1,0:T(8,128)(2,1)S(1)}, u32[]{:S(2)}, u32[]{:S(2)}) collective-permute-start(bf16[32,16,128]{2,1,0:T(8,128)(2,1)S(1)} %get-tuple-element.31), channel_id=1, source_target_pairs={{0,4},{4,0},{8,12},{12,8},{16,20},{20,16},{24,28},{28,24},{32,36},... | collective-permute-start | bytes 393224 | tf_op jit(solution)/shard_map/ppermute | solution.py:356
  76.3 6.2 %collective-permute-start.5 = (f32[16,512]{1,0:T(8,128)S(1)}, f32[16,512]{1,0:T(8,128)S(1)}, u32[]{:S(2)}, u32[]{:S(2)}) collective-permute-start(f32[16,512]{1,0:T(8,128)S(1)} %shard_map.84.mine_ref), channel_id=1, source_target_pairs={{0,2},{1,3},{2,0},{3,1},{4,6},{5,7},{6,4},{7,5},{8,10},{9,11},{10,... | collective-permute-start | bytes 98312 | tf_op jit(solution)/shard_map/ppermute | solution.py:366
  77.7 5.1 %collective-permute-start.6 = (f32[16,512]{1,0:T(8,128)S(1)}, f32[16,512]{1,0:T(8,128)S(1)}, u32[]{:S(2)}, u32[]{:S(2)}) collective-permute-start(f32[16,512]{1,0:T(8,128)S(1)} %shard_map.84.mine_ref), channel_id=1, source_target_pairs={{0,3},{1,2},{2,1},{3,0},{4,7},{5,6},{6,5},{7,4},{8,11},{9,10},{10,... | collective-permute-start | bytes 98312 | tf_op jit(solution)/shard_map/ppermute | solution.py:366
  79.2 3.9 %collective-permute-start.7 = (f32[16,512]{1,0:T(8,128)S(1)}, f32[16,512]{1,0:T(8,128)S(1)}, u32[]{:S(2)}, u32[]{:S(2)}) collective-permute-start(f32[16,512]{1,0:T(8,128)S(1)} %shard_map.84.mine_ref), channel_id=1, source_target_pairs={{0,1},{1,0},{2,3},{3,2},{4,5},{5,4},{6,7},{7,6},{8,9},{9,8},{10,11... | collective-permute-start | bytes 98312 | tf_op jit(solution)/shard_map/ppermute | solution.py:366
